TPU v7x, 512 devices: a whole 4x8x8 slice. The times are simulated.
512 devices in a mesh: fsdp: 128 (over z, y, core), rep: 4 (over x).
Axes of the slice: x: 4, y: 8, z: 8, core: 2. Of those that a mesh axis runs over, the one named last changes fastest.
Arguments:
- replica_grads: bfloat16 [4, 512, 65536], P('rep', 'fsdp'), may hold values from -18 to 18
- momentum: float32 [512, 65536], P('fsdp', 'rep'), may hold values from -6 to 6
- second_moment: float32 [512, 65536], P('fsdp', 'rep'), may hold values from 0.0001 to 1
- factor_stats: float32 [128, 4, 512, 512], P('fsdp', 'rep'), may hold values from -0.1 to 16.2, as said below
- block_owner: int32 [128], replicated, may hold values from 0 to 127, as said below
- block_offset: int32 [128], replicated, may hold values from 0 to 127, each once
Outputs:
- new_momentum: float32 [512, 65536], P('fsdp', 'rep')
- new_second: float32 [512, 65536], P('fsdp', 'rep')
- new_factors: float32 [128, 4, 512, 512], P('fsdp', 'rep')
Inputs may be any that keep to these rules, and one draw needn't show every extreme that they name: `block_owner`: each fsdp index owns at most 2 blocks; exactly 32 indices own two blocks, 64 own one, the others none. `factor_stats`: symmetric.
All inputs are finite; a program needn't handle non-finite values.
Results may differ from a plain program's by a relative error of at most 0.017.
Values may be sent and summed in bfloat16 or wider, within the bound.
A program may use at most 128 MiB of HBM per device.

v0:
```python
import jax
import jax.numpy as jnp
from jax import lax
from jax.sharding import PartitionSpec as P

ITERS = 3


FACTOR_DECAY = 0.95
MATRIX_EPS = 1e-06
ADAM_DECAY = 0.99
ADAM_EPS = 1e-08
NORM_EPS = 1e-06
MOMENTUM_DECAY = 0.9


def matmul_high(left, right):
    return jnp.dot(left, right, precision=lax.Precision.HIGHEST, preferred_element_type=jnp.float32)


def inverse_root(matrix):
    identity = jnp.eye(matrix.shape[0], dtype=jnp.float32)
    frobenius = jnp.sqrt(jnp.sum(matrix * matrix))
    scaling = 2.5 / frobenius
    coupled = scaling * matrix
    iterate = identity
    for section in range(ITERS):
        poly_step = (5.0 * identity - coupled) * 0.25
        if section == 0:
            iterate = jnp.sqrt(jnp.sqrt(scaling)) * poly_step
        else:
            iterate = matmul_high(iterate, poly_step)
        if section + 1 < ITERS:
            squared = matmul_high(poly_step, poly_step)
            coupled = matmul_high(matmul_high(squared, squared), coupled)
    return iterate


def slot_ranks(block_owner):
    positions = jnp.arange(block_owner.shape[0], dtype=jnp.int32)
    same_owner = block_owner[:, None] == block_owner[None, :]
    earlier = positions[None, :] < positions[:, None]
    return jnp.sum((same_owner & earlier).astype(jnp.int32), axis=1)


def shards(replica_grads, momentum, second_moment, factor_stats, block_owner, block_offset):
    fsdp_count = lax.axis_size("fsdp")
    rep_count = lax.axis_size("rep")
    rep_index = lax.axis_index("rep")
    row_count = momentum.shape[0]
    quarter_cols = momentum.shape[1]
    block_size = factor_stats.shape[-1]
    col_count = quarter_cols * rep_count
    block_count = col_count // block_size
    quarter_blocks = block_count // rep_count
    slot_count = rep_count // 2
    target = block_owner * slot_count + slot_ranks(block_owner)
    slot_total = fsdp_count * slot_count
    slot_ids = jnp.arange(slot_total, dtype=jnp.int32)
    matches = target[None, :] == slot_ids[:, None]
    filled = jnp.any(matches, axis=1)
    slot_pos = jnp.sum(jnp.where(matches, block_offset[None, :], 0), axis=1)
    column_ids = jnp.arange(block_count, dtype=jnp.int32)
    at_column = block_offset[None, :] == column_ids[:, None]
    column_slot = jnp.sum(jnp.where(at_column, target[None, :], 0), axis=1)
    own_grad = replica_grads[0].astype(jnp.float32)
    gradient = lax.psum(own_grad.astype(jnp.bfloat16), "rep")
    grad_quarter = lax.dynamic_slice_in_dim(gradient, rep_index * quarter_cols, quarter_cols, 1)
    source = gradient.reshape(row_count, block_count, block_size)
    piece_width = source.shape[2]
    outgoing = jnp.take(source, slot_pos, axis=1)
    outgoing = jnp.where(filled[None, :, None], outgoing, jnp.zeros((), jnp.bfloat16))
    outgoing = outgoing.reshape(row_count, fsdp_count, slot_count * piece_width)
    arrived = lax.all_to_all(outgoing, "fsdp", split_axis=1, concat_axis=0, tiled=True)
    blocks = arrived.reshape(block_size, slot_count, block_size)
    grad_wide = grad_quarter.astype(jnp.float32)
    new_second = ADAM_DECAY * second_moment + (1.0 - ADAM_DECAY) * grad_wide * grad_wide
    adam_dir = grad_wide / (jnp.sqrt(new_second) + ADAM_EPS)
    partial_sq = jnp.sum(
        (adam_dir * adam_dir).reshape(row_count, quarter_blocks, block_size), axis=(0, 2)
    )
    placed = lax.dynamic_update_slice_in_dim(
        jnp.zeros((block_count,), jnp.float32), partial_sq, rep_index * quarter_blocks, 0
    )
    totals = lax.psum(placed, ("fsdp", "rep"))
    my_slot = rep_index // 2
    my_side = rep_index % 2
    my_block = lax.dynamic_index_in_dim(blocks, my_slot, 1, keepdims=False)
    chosen = jnp.where(my_side == 0, my_block, my_block.T)
    statistic = jnp.dot(chosen, chosen.T, preferred_element_type=jnp.float32)
    factor_new = FACTOR_DECAY * factor_stats[0, 0] + (1.0 - FACTOR_DECAY) * statistic
    identity = jnp.eye(block_size, dtype=jnp.float32)
    root_half = inverse_root(factor_new + MATRIX_EPS * identity).astype(jnp.bfloat16)
    roots = lax.all_gather(root_half[None], "rep", axis=0, tiled=True)
    paired = roots.reshape(slot_count, 2, block_size, block_size)
    lefts = paired[:, 0]
    rights = paired[:, 1]
    halfway = jnp.einsum("sij,jsk->sik", lefts, blocks, preferred_element_type=jnp.float32).astype(
        jnp.bfloat16
    )
    precond = jnp.einsum("sij,sjk->isk", halfway, rights, preferred_element_type=jnp.float32)
    prec_sq = jnp.sum(precond * precond, axis=(0, 2))
    my_index = lax.axis_index("fsdp")
    my_slots = my_index * slot_count + jnp.arange(slot_count, dtype=jnp.int32)
    graft_sq = jnp.take(totals, jnp.take(slot_pos, my_slots))
    graft_scale = jnp.sqrt(graft_sq / (prec_sq + NORM_EPS))
    grafted = (precond * graft_scale[None, :, None]).astype(jnp.bfloat16)
    returned = lax.all_to_all(
        grafted.reshape(block_size, 1, slot_count * block_size),
        "fsdp",
        split_axis=0,
        concat_axis=1,
        tiled=True,
    )
    returned = returned.reshape(row_count, slot_total, block_size)
    my_cols = lax.dynamic_slice_in_dim(column_slot, rep_index * quarter_blocks, quarter_blocks, 0)
    update = jnp.take(returned, my_cols, axis=1).reshape(row_count, quarter_cols)
    new_momentum = MOMENTUM_DECAY * momentum + update.astype(jnp.float32)
    return (new_momentum, new_second, factor_new[None, None])


def solution(mesh):
    placed = (
        P("rep", "fsdp", None),
        P("fsdp", "rep"),
        P("fsdp", "rep"),
        P("fsdp", "rep", None, None),
        P(),
        P(),
    )
    return jax.shard_map(
        shards,
        mesh=mesh,
        in_specs=placed,
        out_specs=(P("fsdp", "rep"), P("fsdp", "rep"), P("fsdp", "rep", None, None)),
        check_vma=False,
    )
```

profile of v0, /device:TPU:1, one launch (start us, length us, event | category | flops | bytes accessed | tf_op | source)
XLA Modules:
  0.0 306.6 jit_solution(1251381873039298873)
XLA Ops:
  7.2 0.7 all-reduce.2.cloned.1.call-update
  7.9 0.9 convert_reduce_fusion
  8.8 0.7 multiply_add_fusion
  9.6 0.8 select_reduce_fusion
  11.5 55.9 %all-reduce.2.cloned.1.call-done = bf16[4,65536]{1,0:T(4,128)(2,1)} async-done(((bf16[4,65536]{1,0:T(4,128)(2,1)}), bf16[4,65536]{1,0:T(4,128)(2,1)}) %all-reduce.2.cloned.1.call-update) | async-done | bytes 524304 | tf_op jit(solution)/shard_map/psum | solution.py:67
  67.4 2.6 gather_fusion
  70.0 2.4 select_select_fusion
  72.4 16.4 %all-to-all-start = ((bf16[4,128,1024]{2,0,1:T(4,128)(2,1)}), bf16[4,128,1024]{2,0,1:T(4,128)(2,1)S(1)}, u32[]{:S(2)}, u32[]{:S(2)}) async-start(bf16[4,128,1024]{2,0,1:T(4,128)(2,1)} %select_select_fusion), calls=%async_computation | async-start | bytes 2097152 | tf_op jit(solution)/shard_map/all_to_all | solution.py:74
  88.9 30.8 %all-to-all-done = bf16[4,128,1024]{2,0,1:T(4,128)(2,1)S(1)} async-done(((bf16[4,128,1024]{2,0,1:T(4,128)(2,1)}), bf16[4,128,1024]{2,0,1:T(4,128)(2,1)S(1)}, u32[]{:S(2)}, u32[]{:S(2)}) %all-to-all-start) | async-done | bytes 1048608 | tf_op jit(solution)/shard_map/all_to_all | solution.py:74
  120.1 1.1 constant_dynamic-slice_fusion
  121.2 2.3 copy.57
  123.5 2.8 multiply_reduce_fusion.1
  127.1 2.0 fusion.6
  129.1 1.8 fusion.56
  131.0 1.9 fusion.10
  132.9 1.9 fusion.12
  134.8 3.3 %fusion.8 = f32[512,512]{1,0:T(8,128)S(1)} fusion(f32[512,512]{1,0:T(8,128)S(1)} %fusion.10, f32[]{:T(128)S(6)} %mul.125, f32[]{:T(128)S(6)} %div.24, f32[512,512]{1,0:T(8,128)} %copy-done), kind=kOutput, calls=%fused_computation.21 | convolution fusion | flops 1613496320 | bytes 3145736 | tf_op jit(solution)/shard_map/dot_general | solution.py:18
  138.0 1.8 fusion.57
  139.9 2.1 fusion.2
  142.0 2.7 convolution_convert_fusion.1
  144.7 0.6 gather_fusion.1
  145.4 1.9 fusion.33
  147.7 96.0 %psum.15 = f32[128]{0:T(128)S(1)} all-reduce(f32[128]{0:T(128)S(1)} %dynamic_update_slice.3), channel_id=1, replica_groups=mesh['fsdp'=128,'rep'=4] {'fsdp','rep'}, use_global_device_ids=true, to_apply=%region_8.9 | all-reduce | flops 128 | bytes 1024 | tf_op jit(solution)/shard_map/psum | solution.py:85
  244.3 3.0 multiply_reduce_fusion
  248.2 1.5 reduce.4
  250.2 1.5 reshape.189
  251.7 8.0 %all-to-all-start.1 = ((bf16[128,2,2048]{2,1,0:T(2,128)(2,1)}), bf16[128,2,2048]{2,1,0:T(2,128)(2,1)S(1)}, u32[]{:S(2)}, u32[]{:S(2)}) async-start(bf16[128,2,2048]{2,1,0:T(2,128)(2,1)} %reshape.189), calls=%async_computation.1 | async-start | bytes 2097152 | tf_op jit(solution)/shard_map/all_to_all | solution.py:108
  260.1 30.6 %all-to-all-done.1 = bf16[128,2,2048]{2,1,0:T(2,128)(2,1)S(1)} async-done(((bf16[128,2,2048]{2,1,0:T(2,128)(2,1)}), bf16[128,2,2048]{2,1,0:T(2,128)(2,1)S(1)}, u32[]{:S(2)}, u32[]{:S(2)}) %all-to-all-start.1) | async-done | bytes 1048608 | tf_op jit(solution)/shard_map/all_to_all | solution.py:108
  290.6 1.0 reshape.190
  291.7 6.1 %reduce.3 = bf16[512,1024]{1,0:T(8,128)(2,1)S(1)} reduce(bf16[512,1,1024]{2,1,0:T(2,128)(2,1)S(1)} %reshape.190, bf16[]{:T(256)} %constant.135), dimensions={1}, to_apply=%all_to_all.25.reduce_sub_computation | reduce | bytes 2097154 | tf_op jit(solution)/shard_map/all_to_all | solution.py:108
  298.3 0.7 gather_fusion.3
  299.0 0.8 convert_add_fusion
  (44 shorter events, 4.9 us)
Async XLA Ops:
  7.2 60.2 %all-reduce.2.cloned.1.call-start = ((), (), s32[]{:S(2)}) async-start(), calls=%async_computation.2 | async-start | bytes 1048576 | tf_op jit(solution)/shard_map/psum | solution.py:67
  72.4 47.3 %all-to-all-start = ((bf16[4,128,1024]{2,0,1:T(4,128)(2,1)}), bf16[4,128,1024]{2,0,1:T(4,128)(2,1)S(1)}, u32[]{:S(2)}, u32[]{:S(2)}) async-start(bf16[4,128,1024]{2,0,1:T(4,128)(2,1)} %select_select_fusion), calls=%async_computation | async-start | bytes 2097152 | tf_op jit(solution)/shard_map/all_to_all | solution.py:74
  88.8 155.5 %all-gather.3.cloned.1.call-start = ((), (), s32[]{:S(2)}) async-start(), calls=%async_computation.3 | async-start | bytes 2621440 | tf_op jit(solution)/shard_map/all_gather | solution.py:94
  126.3 4.6 %copy-start = (f32[512,512]{1,0:T(8,128)}, f32[512,512]{1,0:T(8,128)S(1)}, u32[]{:S(2)}) copy-start(f32[512,512]{1,0:T(8,128)S(1)} %get-tuple-element.8) | copy-start | bytes 3145732
  142.0 3.4 %copy-start.1 = (f32[4,16384]{1,0:T(4,128)S(1)}, f32[4,16384]{1,0:T(4,128)}, u32[]{:S(2)}) copy-start(f32[4,16384]{1,0:T(4,128)} %param.8) | copy-start | bytes 786436
  250.2 9.5 %copy-start.3 = (s32[128]{0:T(128)S(1)}, s32[128]{0:T(128)}, u32[]{:S(2)}) copy-start(s32[128]{0:T(128)} %param.11) | copy-start | bytes 1540
  251.7 38.9 %all-to-all-start.1 = ((bf16[128,2,2048]{2,1,0:T(2,128)(2,1)}), bf16[128,2,2048]{2,1,0:T(2,128)(2,1)S(1)}, u32[]{:S(2)}, u32[]{:S(2)}) async-start(bf16[128,2,2048]{2,1,0:T(2,128)(2,1)} %reshape.189), calls=%async_computation.1 | async-start | bytes 2097152 | tf_op jit(solution)/shard_map/all_to_all | solution.py:108
  291.7 7.3 %copy-start.2 = (f32[4,16384]{1,0:T(4,128)S(1)}, f32[4,16384]{1,0:T(4,128)}, u32[]{:S(2)}) copy-start(f32[4,16384]{1,0:T(4,128)} %param.7) | copy-start | bytes 786436
Sparse Core Ops, SparseCore 0:
  10.3 57.0 all-reduce.1
  144.8 29.0 all-gather.2
where the time goes:
time: 307 us
  waiting for transfers between devices  118 us (38%)
  blocking collectives  96 us (31%)
  starting transfers between devices  24.5 us (8%)
  matrix products  23.3 us (8%)
  other arithmetic  15.9 us (5%)
  between operations  15.2 us (5%)
  local copies, waits for them, and re-layouts  13.8 us (4%)
    psum x1, blocking collectives, shards(): totals = lax.psum(placed, ('fsdp', 'rep'))  96 us
    psum x1, waiting for transfers between devices, shards(): gradient = lax.psum(own_grad.astype(jnp.bfloat16), 'rep')  55.9 us
    all_to_all x1, waiting for transfers between devices, shards(): lax.all_to_all(outgoing, 'fsdp', split_axis=1, concat_axis=0, tiled=True)  30.8 us
    all_to_all x1, waiting for transfers between devices, shards(): lax.all_to_all(grafted.reshape(block_size, 1, slot_count * block_size), '...  30.6 us
    dot_general x8, matrix products, matmul_high(): jnp.dot(left, right, precision=lax.Precision.HIGHEST, preferred_element_t...  17.5 us
    all_to_all x1, starting transfers between devices, shards(): lax.all_to_all(outgoing, 'fsdp', split_axis=1, concat_axis=0, tiled=True)  16.4 us
    all_to_all x1, starting transfers between devices, shards(): lax.all_to_all(grafted.reshape(block_size, 1, slot_count * block_size), '...  8 us
  transfers between devices with their start and end apart: 4, of which 3 were waited for; matrix products, arithmetic and copies ran while one was open for 2% of the time, Pallas kernels for 0%

commit v1 on v0

v1 whole, which is shorter than its diff:
```python
import jax
import jax.numpy as jnp
from jax import lax
from jax.experimental import pallas as pl
from jax.experimental.pallas import tpu as pltpu
from jax.sharding import PartitionSpec as P

FACTOR_DECAY = 0.95
MATRIX_EPS = 1e-06
ADAM_DECAY = 0.99
ADAM_EPS = 1e-08
NORM_EPS = 1e-06
MOMENTUM_DECAY = 0.9

NF = 128
NR = 4
BS = 512
NBLK = 128
QB = NBLK // NR
HALF = NF // 2
MESH = pl.DeviceIdType.MESH
F32 = jnp.float32
BF16 = jnp.bfloat16


def dot32(left, right):
    return jnp.dot(left, right, preferred_element_type=F32)


def outer_left(mat):
    return lax.dot_general(mat, mat, (((1,), (1,)), ((), ())), preferred_element_type=F32)


def outer_right(mat):
    return lax.dot_general(mat, mat, (((0,), (0,)), ((), ())), preferred_element_type=F32)


def eye_mask():
    return lax.broadcasted_iota(jnp.int32, (BS, BS), 0) == lax.broadcasted_iota(
        jnp.int32, (BS, BS), 1
    )


def plus_diag(mat, value):
    return mat + jnp.where(eye_mask(), value, 0.0)


def roots_of(mats):
    norms = [jnp.sum(jnp.sum(m * m, axis=0, keepdims=True), axis=1, keepdims=True) for m in mats]
    scales = [2.5 / jnp.sqrt(n) for n in norms]
    coupled0 = [z * m for z, m in zip(scales, mats)]

    def next_coupled(coupled, rounded):
        square = [dot32(m, m) for m in rounded]
        inner = [s * 0.0625 - 0.625 * m for s, m in zip(square, coupled)]
        inner_b = [e.astype(BF16) for e in inner]
        fourth = [dot32(e, e) for e in inner_b]
        rest = [(q + 3.125 * e).astype(BF16) for q, e in zip(fourth, inner)]
        return [
            dot32(w, m) + (625.0 / 256.0) * c for w, m, c in zip(rest, rounded, coupled)
        ]

    rounded0 = [m.astype(BF16) for m in coupled0]
    coupled1 = next_coupled(coupled0, rounded0)
    rounded1 = [m.astype(BF16) for m in coupled1]
    pair = [
        (dot32(a, b) - 5.0 * (c + d)) * 0.0625
        for a, b, c, d in zip(rounded0, rounded1, coupled0, coupled1)
    ]
    coupled2 = next_coupled(coupled1, rounded1)
    out = []
    for u, m, z in zip(pair, coupled2, scales):
        last = 5.0 * u - (25.0 / 16.0) * m - dot32(u.astype(BF16), m.astype(BF16))
        root = plus_diag(last * 0.25, 125.0 / 64.0) * jnp.sqrt(jnp.sqrt(z))
        out.append(root.astype(BF16))
    return out


def kernel(
    tab,
    grads,
    mom_in,
    sec_in,
    fac_in,
    newmom_out,
    newsec_out,
    newfac_out,
    mom,
    sec,
    fac,
    newmom,
    newsec,
    newfac,
    gq,
    rs,
    full,
    out,
    arrived,
    block,
    block_x,
    fac_b,
    fac_x,
    ret,
    retbuf,
    xs,
    xr,
    prow,
    zbuf,
    yrow,
    ybuf,
    crow,
    cbuf,
    lsem,
    osem,
    rs_s,
    rs_r,
    ag_s,
    ag_r,
    fx_s,
    fx_r,
    gx_s,
    gx_r,
    a_s,
    a_r,
    b_s,
    b_r,
    x_s,
    x_r,
    z_s,
    z_r,
    y_s,
    y_r,
    c_s,
    c_r,
):
    f = lax.axis_index("fsdp")
    r = lax.axis_index("rep")
    par = lax.rem(r, 2)
    slot = lax.div(r, 2)
    partner = r + 1 - 2 * par
    f_par = lax.rem(f, 2)
    my_j = lax.div(f, 2)
    primary = f_par == par
    other = f_par != par

    def remote(src, dst, send, recv, device):
        return pltpu.make_async_remote_copy(
            src_ref=src,
            dst_ref=dst,
            send_sem=send,
            recv_sem=recv,
            device_id=device,
            device_id_type=MESH,
        )

    def ahead(d):
        return lax.rem(r + d, NR)

    def behind(d):
        return lax.rem(r + NR - d, NR)

    load_g = pltpu.make_async_copy(grads.at[pl.ds(r * QB, QB)], gq, lsem.at[0])
    load_sec = pltpu.make_async_copy(sec_in, sec, lsem.at[1])
    load_fac = pltpu.make_async_copy(fac_in, fac, lsem.at[2])
    load_mom = pltpu.make_async_copy(mom_in, mom, lsem.at[3])
    load_g.start()
    load_sec.start()
    load_fac.start()
    load_mom.start()

    barrier = pltpu.get_barrier_semaphore()
    for d in range(1, NR):
        pl.semaphore_signal(barrier, inc=1, device_id=(f, ahead(d)), device_id_type=MESH)

    def greet(t, carry):
        pl.semaphore_signal(
            barrier, inc=1, device_id=(lax.rem(f + t, NF), r), device_id_type=MESH
        )
        return carry

    lax.fori_loop(1, NF, greet, 0)
    pl.semaphore_wait(barrier, NF - 1 + NR - 1)

    rs_copies = []
    for d in range(1, NR):
        copy = remote(
            grads.at[pl.ds(ahead(d) * QB, QB)],
            rs.at[d - 1],
            rs_s.at[d - 1],
            rs_r.at[d - 1],
            (f, ahead(d)),
        )
        copy.start()
        rs_copies.append(copy)
    load_fac.wait()

    @pl.when(other)
    def _():
        fac_b[...] = fac[...].astype(BF16)

    load_g.wait()
    for copy in rs_copies:
        copy.wait_recv()
    total = gq[...].astype(F32)
    for d in range(1, NR):
        total = total + rs[d - 1].astype(F32)
    mine = total.astype(BF16)
    full[pl.ds(r * QB, QB)] = mine

    for d in range(1, NR):
        remote(
            full.at[pl.ds(r * QB, QB)],
            full.at[pl.ds(r * QB, QB)],
            ag_s.at[d - 1],
            ag_r.at[d - 1],
            (f, ahead(d)),
        ).start()

    @pl.when(other)
    def _():
        remote(fac_b, fac_x, fx_s, fx_r, (f, partner)).start()

    load_sec.wait()
    wide = mine.astype(F32)
    second = ADAM_DECAY * sec[...] + (1.0 - ADAM_DECAY) * wide * wide
    newsec[...] = second
    store_sec = pltpu.make_async_copy(newsec, newsec_out, osem.at[0])
    store_sec.start()
    direction = wide / (jnp.sqrt(second) + ADAM_EPS)
    lanes = jnp.sum(direction * direction, axis=1)
    sums = jnp.sum(lanes, axis=1, keepdims=True)
    diagonal = lax.broadcasted_iota(jnp.int32, (QB, 128), 0) == lax.broadcasted_iota(
        jnp.int32, (QB, 128), 1
    )
    row = jnp.sum(jnp.where(diagonal, sums, 0.0), axis=0, keepdims=True)
    prow[...] = jnp.broadcast_to(row, (8, 128))
    for d in range(1, 8):
        remote(
            prow,
            zbuf.at[d - 1],
            z_s.at[d - 1],
            z_r.at[d - 1],
            (lax.rem(f + 16 * d, NF), r),
        ).start()

    for d in range(1, NR):
        part = full.at[pl.ds(behind(d) * QB, QB)]
        remote(part, part, ag_s.at[d - 1], ag_r.at[d - 1], (f, ahead(d))).wait_recv()

    def send_chunk(t, carry):
        j = lax.rem(my_j + t, HALF)
        owner = 2 * j + par
        column = jnp.maximum(tab[2 * owner + slot], 0)

        @pl.when(owner != f)
        def _():
            out[j] = full[column]
            remote(out.at[j], arrived.at[f], a_s, a_r, (owner, r)).start()

        @pl.when(owner == f)
        def _():
            arrived[f] = full[column]

        return carry

    lax.fori_loop(0, HALF, send_chunk, 0)

    for d in range(1, 8):
        remote(
            prow, zbuf.at[d - 1], z_s.at[d - 1], z_r.at[d - 1], (lax.rem(f + 16 * d, NF), r)
        ).wait()
    acc = prow[...]
    for d in range(1, 8):
        acc = acc + zbuf[d - 1]
    yrow[...] = acc
    low = lax.rem(f, 16)
    for d in range(1, 8):
        remote(
            yrow,
            ybuf.at[d - 1],
            y_s.at[d - 1],
            y_r.at[d - 1],
            (f - low + lax.rem(low + 2 * d, 16), r),
        ).start()

    weight = jnp.where(tab[2 * f + slot] >= 0, 1.0 - FACTOR_DECAY, 0.0)

    @pl.when(primary)
    def _():
        remote(
            arrived.at[pl.ds(0, NF - 1)],
            arrived.at[pl.ds(0, NF - 1)],
            a_s,
            a_r,
            (f, partner),
        ).wait_recv()
        row_id = lax.broadcasted_iota(jnp.int32, (256, 256), 0)
        col_id = lax.broadcasted_iota(jnp.int32, (256, 256), 1)
        gather_id = ((row_id >> 2) & 15) * 16 + (row_id >> 6) * 4 + (row_id & 3)
        perm = jnp.where(col_id == gather_id, 1.0, 0.0).astype(BF16)
        for g in range(8):
            moved = dot32(perm, arrived[pl.ds(16 * g, 16)].reshape(256, 128)).astype(BF16)
            for q in range(4):
                block[pl.ds(64 * g, 64), pl.ds(128 * q, 128)] = moved[64 * q : 64 * q + 64]
        remote(block, block_x, gx_s, gx_r, (f, partner)).start()
        remote(fac_b, fac_x, fx_s, fx_r, (f, partner)).wait_recv()
        grad = block[...]
        own = fac[...]
        theirs = fac_x[...].astype(F32)
        is_left = par == 0
        left = FACTOR_DECAY * jnp.where(is_left, own, theirs) + weight * outer_left(grad)
        right = FACTOR_DECAY * jnp.where(is_left, theirs, own) + weight * outer_right(grad)
        newfac[...] = jnp.where(is_left, left, right)
        pltpu.make_async_copy(newfac, newfac_out, osem.at[1]).start()
        left_root, right_root = roots_of(
            [plus_diag(left, MATRIX_EPS), plus_diag(right, MATRIX_EPS)]
        )
        halfway = dot32(left_root, grad).astype(BF16)
        precond = dot32(halfway, right_root)
        prec_sq = jnp.sum(
            jnp.sum(precond * precond, axis=0, keepdims=True), axis=1, keepdims=True
        )
        unit = (precond * (1.0 / jnp.sqrt(prec_sq + NORM_EPS))).astype(BF16)
        scatter_id = ((row_id >> 2) & 3) * 64 + (row_id >> 4) * 4 + (row_id & 3)
        perm_back = jnp.where(col_id == scatter_id, 1.0, 0.0).astype(BF16)
        for g in range(8):
            piece = jnp.concatenate(
                [unit[64 * g : 64 * g + 64, 128 * q : 128 * q + 128] for q in range(4)], axis=0
            )
            ret[pl.ds(16 * g, 16)] = dot32(perm_back, piece).astype(BF16).reshape(16, 16, 128)

        def send_back(t, carry):
            target = lax.rem(f + t, NF)
            remote(ret.at[target], retbuf.at[my_j], b_s, b_r, (target, r)).start()
            return carry

        lax.fori_loop(1, NF, send_back, 0)
        retbuf[my_j] = ret[f]

    @pl.when(other)
    def _():
        remote(block, block_x, gx_s, gx_r, (f, partner)).wait_recv()
        grad = block_x[...]

        @pl.when(par == 0)
        def _():
            newfac[...] = FACTOR_DECAY * fac[...] + weight * outer_left(grad)

        @pl.when(par == 1)
        def _():
            newfac[...] = FACTOR_DECAY * fac[...] + weight * outer_right(grad)

        pltpu.make_async_copy(newfac, newfac_out, osem.at[1]).start()

    for d in range(1, 8):
        remote(
            yrow,
            ybuf.at[d - 1],
            y_s.at[d - 1],
            y_r.at[d - 1],
            (f - low + lax.rem(low + 2 * d, 16), r),
        ).wait()
    acc = yrow[...]
    for d in range(1, 8):
        acc = acc + ybuf[d - 1]
    crow[...] = acc
    core_copy = remote(crow, cbuf, c_s, c_r, (f + 1 - 2 * f_par, r))
    core_copy.start()

    @pl.when(primary)
    def _():
        part = retbuf.at[pl.ds(0, HALF - 1)]
        remote(part, part, b_s, b_r, (f, partner)).wait_recv()

    @pl.when(other)
    def _():
        remote(retbuf, retbuf, b_s, b_r, (f, partner)).wait_recv()

    for d in range(1, NR):
        base = ahead(d) * QB

        def pack(p, carry, d=d, base=base):
            xs[d - 1, p] = retbuf[tab[2 * NF + base + p] >> 2]
            return carry

        lax.fori_loop(0, QB, pack, 0)
        remote(xs.at[d - 1], xr.at[r], x_s.at[d - 1], x_r.at[d - 1], (f, ahead(d))).start()

    def pack_own(p, carry):
        xr[r, p] = retbuf[tab[2 * NF + r * QB + p] >> 2]
        return carry

    lax.fori_loop(0, QB, pack_own, 0)

    core_copy.wait()
    total_row = (crow[...] + cbuf[...])[0:1]
    scale = jnp.sqrt(
        jnp.sum(jnp.where(diagonal, total_row, 0.0), axis=1, keepdims=True)
    )
    load_mom.wait()
    decayed = MOMENTUM_DECAY * mom[...]
    newmom[...] = decayed
    for d in range(1, NR):
        part = xr.at[behind(d)]
        remote(xs.at[d - 1], part, x_s.at[d - 1], x_r.at[d - 1], (f, ahead(d))).wait_recv()
    for p in range(QB):
        s = tab[2 * NF + r * QB + p]
        holder = 2 * (s & 1) + ((s >> 1) & 1)
        newmom[p] = newmom[p] + xr[holder, p].astype(F32) * scale[p : p + 1]
    store_mom = pltpu.make_async_copy(newmom, newmom_out, osem.at[2])
    store_mom.start()

    for copy in rs_copies:
        copy.wait_send()
    for d in range(1, NR):
        part = full.at[pl.ds(r * QB, QB)]
        remote(part, part, ag_s.at[d - 1], ag_r.at[d - 1], (f, ahead(d))).wait_send()
        remote(xs.at[d - 1], xr.at[r], x_s.at[d - 1], x_r.at[d - 1], (f, ahead(d))).wait_send()

    @pl.when(primary)
    def _():
        part = out.at[pl.ds(0, HALF - 1)]
        remote(part, part, a_s, a_r, (f, partner)).wait_send()
        part_b = ret.at[pl.ds(0, NF - 1)]
        remote(part_b, part_b, b_s, b_r, (f, partner)).wait_send()
        remote(block, block_x, gx_s, gx_r, (f, partner)).wait_send()

    @pl.when(other)
    def _():
        remote(out, out, a_s, a_r, (f, partner)).wait_send()
        remote(fac_b, fac_x, fx_s, fx_r, (f, partner)).wait_send()

    store_sec.wait()
    pltpu.make_async_copy(newfac, newfac_out, osem.at[1]).wait()
    store_mom.wait()


def tables(block_owner, block_offset):
    count = block_owner.shape[0]
    positions = jnp.arange(count, dtype=jnp.int32)
    same = block_owner[:, None] == block_owner[None, :]
    earlier = positions[None, :] < positions[:, None]
    rank = jnp.sum((same & earlier).astype(jnp.int32), axis=1)
    target = block_owner * 2 + rank
    slots = jnp.arange(2 * NF, dtype=jnp.int32)
    slot_column = (
        jnp.sum(jnp.where(target[None, :] == slots[:, None], block_offset[None, :] + 1, 0), axis=1)
        - 1
    )
    at_column = block_offset[None, :] == positions[:, None]
    column_slot = jnp.sum(jnp.where(at_column, target[None, :], 0), axis=1)
    return jnp.concatenate([slot_column, column_slot])


def chunked(array):
    columns = array.shape[1]
    tiles = array.reshape(4, columns // 128, 128).transpose(1, 0, 2)
    return tiles.reshape(columns // 512, 16, 128)


def unchunked(array):
    count = array.shape[0]
    return array.reshape(count * 4, 4, 128).transpose(1, 0, 2).reshape(4, count * 512)


def shards(replica_grads, momentum, second_moment, factor_stats, block_owner, block_offset):
    tab = tables(block_owner, block_offset)
    any_space = pl.BlockSpec(memory_space=pl.ANY)
    dma = pltpu.SemaphoreType.DMA
    outs = pl.pallas_call(
        kernel,
        out_shape=(
            jax.ShapeDtypeStruct((QB, 16, 128), F32),
            jax.ShapeDtypeStruct((QB, 16, 128), F32),
            jax.ShapeDtypeStruct((BS, BS), F32),
        ),
        in_specs=[pl.BlockSpec(memory_space=pltpu.SMEM)] + [any_space] * 4,
        out_specs=(any_space,) * 3,
        scratch_shapes=[
            pltpu.VMEM((QB, 16, 128), F32),
            pltpu.VMEM((QB, 16, 128), F32),
            pltpu.VMEM((BS, BS), F32),
            pltpu.VMEM((QB, 16, 128), F32),
            pltpu.VMEM((QB, 16, 128), F32),
            pltpu.VMEM((BS, BS), F32),
            pltpu.VMEM((QB, 16, 128), BF16),
            pltpu.VMEM((NR - 1, QB, 16, 128), BF16),
            pltpu.VMEM((NBLK, 16, 128), BF16),
            pltpu.VMEM((HALF, 16, 128), BF16),
            pltpu.VMEM((NF, 16, 128), BF16),
            pltpu.VMEM((BS, BS), BF16),
            pltpu.VMEM((BS, BS), BF16),
            pltpu.VMEM((BS, BS), BF16),
            pltpu.VMEM((BS, BS), BF16),
            pltpu.VMEM((NF, 16, 128), BF16),
            pltpu.VMEM((HALF, 16, 128), BF16),
            pltpu.VMEM((NR - 1, QB, 16, 128), BF16),
            pltpu.VMEM((NR, QB, 16, 128), BF16),
            pltpu.VMEM((8, 128), F32),
            pltpu.VMEM((7, 8, 128), F32),
            pltpu.VMEM((8, 128), F32),
            pltpu.VMEM((7, 8, 128), F32),
            pltpu.VMEM((8, 128), F32),
            pltpu.VMEM((8, 128), F32),
            dma((4,)),
            dma((3,)),
            dma((3,)),
            dma((3,)),
            dma((3,)),
            dma((3,)),
            dma,
            dma,
            dma,
            dma,
            dma,
            dma,
            dma,
            dma,
            dma((3,)),
            dma((3,)),
            dma((7,)),
            dma((7,)),
            dma((7,)),
            dma((7,)),
            dma,
            dma,
        ],
        compiler_params=pltpu.CompilerParams(
            collective_id=0, has_side_effects=True, vmem_limit_bytes=48 * 1024 * 1024
        ),
    )(
        tab,
        chunked(replica_grads[0]),
        chunked(momentum),
        chunked(second_moment),
        factor_stats[0, 0],
    )
    new_momentum, new_second, new_factors = outs
    return (unchunked(new_momentum), unchunked(new_second), new_factors[None, None])


def solution(mesh):
    placed = (
        P("rep", "fsdp", None),
        P("fsdp", "rep"),
        P("fsdp", "rep"),
        P("fsdp", "rep", None, None),
        P(),
        P(),
    )
    return jax.shard_map(
        shards,
        mesh=mesh,
        in_specs=placed,
        out_specs=(P("fsdp", "rep"), P("fsdp", "rep"), P("fsdp", "rep", None, None)),
        check_vma=False,
    )
```

time: 307 us -> 81.5 us (0.27)
  waiting for transfers between devices: 118 us -> 0 us
  blocking collectives: 96 us -> 0 us
  Pallas kernels: 0 us -> 72.5 us
  starting transfers between devices: 24.5 us -> 0 us
  matrix products: 23.3 us -> 0 us
  other arithmetic: 15.9 us -> 0.41 us
  between operations: 15.2 us -> 0.69 us
  local copies, waits for them, and re-layouts: 13.8 us -> 7.67 us
    psum x1 -> x0, blocking collectives: 96 us -> none  [shards(): totals = lax.psum(placed, ('fsdp', 'rep'))]
    pallas_call x0 -> x1, Pallas kernels: none -> 72.5 us  [shards(): pl.pallas_call(kernel, out_shape=(jax.ShapeDtypeStruct((QB, 16, 128), F32...]
    all_to_all x2 -> x0, waiting for transfers between devices: 61.4 us -> none  [the longest x1 30.8 us: shards(): lax.all_to_all(outgoing, 'fsdp', split_axis=1, concat_axis=0, tiled=True)]
    psum x1 -> x0, waiting for transfers between devices: 55.9 us -> none  [shards(): gradient = lax.psum(own_grad.astype(jnp.bfloat16), 'rep')]
    all_to_all x2 -> x0, starting transfers between devices: 24.4 us -> none  [the longest x1 16.4 us: shards(): lax.all_to_all(outgoing, 'fsdp', split_axis=1, concat_axis=0, tiled=True)]
    dot_general x10 -> x0, matrix products: 23.3 us -> none  [the longest x8 17.5 us: matmul_high(): jnp.dot(left, right, precision=lax.Precision.HIGHEST, preferred_element_t...]
    all_to_all x1 -> x0, other arithmetic: 6.14 us -> none  [shards(): lax.all_to_all(grafted.reshape(block_size, 1, slot_count * block_size), '...]
    gather x4 -> x0, local copies, waits for them, and re-layouts: 4.52 us -> none  [the longest x1 2.58 us: shards(): outgoing = jnp.take(source, slot_pos, axis=1)]
  transfers between devices with their start and end apart: 4 -> 0, of which waited for: 3 -> 0; matrix products, arithmetic and copies ran while one was open for 2% -> 0% of each run, Pallas kernels for 0% -> 0%
where the time goes in v1:
time: 81.5 us; the launch traced here: 81.2 us
  Pallas kernels  72.5 us (89%)
  local copies, waits for them, and re-layouts  7.67 us (9%)
    pallas_call x1, Pallas kernels, shards(): pl.pallas_call(kernel, out_shape=(jax.ShapeDtypeStruct((QB, 16, 128), F32...  72.5 us
    unnamed x15, local copies, waits for them, and re-layouts  7.67 us

profile of v1, /device:TPU:1, one launch (start us, length us, event | category | flops | bytes accessed | tf_op | source)
XLA Modules:
  0.0 81.2 jit_solution(8417262801176447983)
XLA Ops:
  0.6 0.0 copy-start.4
  0.6 0.6 copy-done.4
  1.3 0.0 copy-start.5
  1.3 0.2 convert_reduce_fusion
  1.5 0.5 copy-done.5
  1.9 0.1 select_reduce_fusion
  2.1 0.1 select_reduce_fusion.1
  2.2 0.0 copy-start
  2.2 1.2 %copy-done = f32[1,1,512,512]{3,2,1,0:T(8,128)S(1)} copy-done((f32[1,1,512,512]{3,2,1,0:T(8,128)S(1)}, f32[1,1,512,512]{3,2,1,0:T(8,128)}, u32[]{:S(2)}) %copy-start) | copy-done | bytes 1048600
  3.4 0.0 copy-start.1
  3.4 1.0 %copy-done.1 = bf16[1,4,65536]{2,1,0:T(4,128)(2,1)S(1)} copy-done((bf16[1,4,65536]{2,1,0:T(4,128)(2,1)S(1)}, bf16[1,4,65536]{2,1,0:T(4,128)(2,1)}, u32[]{:S(2)}) %copy-start.1) | copy-done | bytes 524312
  4.5 0.0 copy-start.2
  4.5 0.9 %copy-done.2 = f32[4,16384]{1,0:T(4,128)S(1)} copy-done((f32[4,16384]{1,0:T(4,128)S(1)}, f32[4,16384]{1,0:T(4,128)}, u32[]{:S(2)}) %copy-start.2) | copy-done | bytes 262168
  5.4 0.0 copy-start.3
  5.4 0.9 %copy-done.3 = f32[4,16384]{1,0:T(4,128)S(1)} copy-done((f32[4,16384]{1,0:T(4,128)S(1)}, f32[4,16384]{1,0:T(4,128)}, u32[]{:S(2)}) %copy-start.3) | copy-done | bytes 262168
  6.4 72.5 %shard_map.85 = (f32[32,16,128]{2,1,0:T(8,128)S(1)}, f32[32,16,128]{2,1,0:T(8,128)S(1)}, f32[512,512]{1,0:T(8,128)S(1)}) custom-call(s32[384]{0:T(512)S(1)} %pad_add_fusion.tab, bf16[128,16,128]{2,1,0:T(8,128)(2,1)S(1)} %bitcast.29, f32[32,16,128]{2,1,0:T(8,128)S(1)} %bitcast.30, f32[32,16,128]{2,1,0:T(8,128)S(1)} %bitcast.31, f32[512,512]{1,0:T(8,128)S(1)} %bitcast.27), custom_call_target="tpu_custom_call" | custom-call | tf_op jit(solution)/shard_map/pallas_call | solution.py:470
  78.9 0.7 copy.22
  79.6 0.7 copy.23
  80.3 1.0 %copy.24 = f32[1,1,512,512]{3,2,1,0:T(8,128)} copy(f32[1,1,512,512]{3,2,1,0:T(8,128)S(1)} %bitcast.28) | data formatting | bytes 2097152
  (3 shorter events, 0.0 us)
Async XLA Ops:
  0.6 0.7 copy-start.4
  1.3 0.7 copy-start.5
  2.2 1.2 %copy-start = (f32[1,1,512,512]{3,2,1,0:T(8,128)S(1)}, f32[1,1,512,512]{3,2,1,0:T(8,128)}, u32[]{:S(2)}) copy-start(f32[1,1,512,512]{3,2,1,0:T(8,128)} %param.9) | copy-start | bytes 3145732
  3.4 1.0 %copy-start.1 = (bf16[1,4,65536]{2,1,0:T(4,128)(2,1)S(1)}, bf16[1,4,65536]{2,1,0:T(4,128)(2,1)}, u32[]{:S(2)}) copy-start(bf16[1,4,65536]{2,1,0:T(4,128)(2,1)} %param.6) | copy-start | bytes 1572868
  4.5 0.9 %copy-start.2 = (f32[4,16384]{1,0:T(4,128)S(1)}, f32[4,16384]{1,0:T(4,128)}, u32[]{:S(2)}) copy-start(f32[4,16384]{1,0:T(4,128)} %param.7) | copy-start | bytes 786436
  5.4 0.9 %copy-start.3 = (f32[4,16384]{1,0:T(4,128)S(1)}, f32[4,16384]{1,0:T(4,128)}, u32[]{:S(2)}) copy-start(f32[4,16384]{1,0:T(4,128)} %param.8) | copy-start | bytes 786436

commit v2 on v1

v2 whole, which is shorter than its diff:
```python
import jax
import jax.numpy as jnp
from jax import lax
from jax.experimental import pallas as pl
from jax.experimental.pallas import tpu as pltpu
from jax.sharding import PartitionSpec as P

FACTOR_DECAY = 0.95
MATRIX_EPS = 1e-06
ADAM_DECAY = 0.99
ADAM_EPS = 1e-08
NORM_EPS = 1e-06
MOMENTUM_DECAY = 0.9

NF = 128
NR = 4
BS = 512
NBLK = 128
QB = NBLK // NR
HALF = NF // 2
PARTS = 2
PB = QB // PARTS
NZ = 8
MESH = pl.DeviceIdType.MESH
F32 = jnp.float32
BF16 = jnp.bfloat16


def dot32(left, right):
    return jnp.dot(left, right, preferred_element_type=F32)


def outer_left(mat):
    return lax.dot_general(mat, mat, (((1,), (1,)), ((), ())), preferred_element_type=F32)


def outer_right(mat):
    return lax.dot_general(mat, mat, (((0,), (0,)), ((), ())), preferred_element_type=F32)


def eye_mask():
    return lax.broadcasted_iota(jnp.int32, (BS, BS), 0) == lax.broadcasted_iota(
        jnp.int32, (BS, BS), 1
    )


def plus_diag(mat, value):
    return mat + jnp.where(eye_mask(), value, 0.0)


def roots_of(mats):
    norms = [jnp.sum(jnp.sum(m * m, axis=0, keepdims=True), axis=1, keepdims=True) for m in mats]
    scales = [2.5 / jnp.sqrt(n) for n in norms]
    coupled0 = [z * m for z, m in zip(scales, mats)]

    def next_coupled(coupled, rounded):
        square = [dot32(m, m) for m in rounded]
        inner = [s * 0.0625 - 0.625 * m for s, m in zip(square, coupled)]
        inner_b = [e.astype(BF16) for e in inner]
        fourth = [dot32(e, e) for e in inner_b]
        rest = [(q + 3.125 * e).astype(BF16) for q, e in zip(fourth, inner)]
        return [
            dot32(w, m) + (625.0 / 256.0) * c for w, m, c in zip(rest, rounded, coupled)
        ]

    rounded0 = [m.astype(BF16) for m in coupled0]
    coupled1 = next_coupled(coupled0, rounded0)
    rounded1 = [m.astype(BF16) for m in coupled1]
    pair = [
        (dot32(a, b) - 5.0 * (c + d)) * 0.0625
        for a, b, c, d in zip(rounded0, rounded1, coupled0, coupled1)
    ]
    coupled2 = next_coupled(coupled1, rounded1)
    out = []
    for u, m, z in zip(pair, coupled2, scales):
        last = 5.0 * u - (25.0 / 16.0) * m - dot32(u.astype(BF16), m.astype(BF16))
        root = plus_diag(last * 0.25, 125.0 / 64.0) * jnp.sqrt(jnp.sqrt(z))
        out.append(root.astype(BF16))
    return out


def tables(owner, offset):
    above = lax.broadcasted_iota(jnp.int32, (NBLK, NBLK), 0)
    across = lax.broadcasted_iota(jnp.int32, (NBLK, NBLK), 1)

    def down(row):
        return jnp.broadcast_to(row, (NBLK, NBLK)).T

    same = (down(owner) == owner) & (above < across)
    target = 2 * owner + jnp.sum(jnp.where(same, 1, 0), axis=0, keepdims=True)
    target_down, offset_down = down(target), down(offset)
    rows = [
        jnp.sum(jnp.where(target_down == across + NBLK * h, offset_down + 1, 0), axis=0, keepdims=True)
        - 1
        for h in range(2)
    ]
    slot_of = jnp.sum(jnp.where(offset_down == across, target_down, 0), axis=0, keepdims=True)
    rows.append(jnp.minimum(slot_of, 2 * NF - 1))
    return rows


def kernel(
    owner_in,
    offset_in,
    grads,
    mom_in,
    sec_in,
    fac_in,
    newmom_out,
    newsec_out,
    newfac_out,
    mom,
    sec,
    fac,
    newmom,
    newsec,
    newfac,
    gv,
    gq,
    rs,
    full,
    out,
    comb,
    arrived,
    block,
    block_x,
    fac_b,
    fac_x,
    unit_s,
    ret,
    retpair,
    xs,
    xr,
    prow,
    zrow,
    zbuf,
    yrow,
    ybuf,
    trow,
    cbuf,
    tabv,
    tab,
    tsem,
    lsem,
    osem,
    rs_s,
    rs_r,
    ag_s,
    ag_r,
    fx_s,
    fx_r,
    gx_s,
    gx_r,
    a_s,
    a_r,
    m_s,
    m_r,
    l_s,
    l_r,
    b_s,
    b_r,
    t_s,
    t_r,
    x_s,
    x_r,
    z_s,
    z_r,
    y_s,
    y_r,
    c_s,
    c_r,
):
    f = lax.axis_index("fsdp")
    r = lax.axis_index("rep")
    par = lax.rem(r, 2)
    slot = lax.div(r, 2)
    partner = r + 1 - 2 * par
    f_par = lax.rem(f, 2)
    my_j = lax.div(f, 2)
    my_z = lax.div(f, 2 * NZ)
    my_y = lax.rem(lax.div(f, 2), NZ)
    mate = f + 1 - 2 * f_par
    primary = f_par == par
    other = f_par != par

    def remote(src, dst, send, recv, device):
        return pltpu.make_async_remote_copy(
            src_ref=src,
            dst_ref=dst,
            send_sem=send,
            recv_sem=recv,
            device_id=device,
            device_id_type=MESH,
        )

    def on_z(d):
        return lax.rem(my_z + d, NZ)

    def on_y(d):
        return lax.rem(my_y + d, NZ)

    def along_z(d):
        return (2 * NZ * on_z(d) + 2 * my_y + f_par, r)

    def along_y(d):
        return (2 * NZ * my_z + 2 * on_y(d) + f_par, r)

    def ahead(d):
        return lax.rem(r + d, NR)

    def behind(d):
        return lax.rem(r + NR - d, NR)

    load_g = pltpu.make_async_copy(grads, gv, lsem.at[0])
    load_sec = pltpu.make_async_copy(sec_in, sec, lsem.at[1])
    load_fac = pltpu.make_async_copy(fac_in, fac, lsem.at[2])
    load_mom = pltpu.make_async_copy(mom_in, mom, lsem.at[3])
    load_g.start()
    load_sec.start()
    load_fac.start()
    load_mom.start()

    barrier = pltpu.get_barrier_semaphore()

    def greet(device):
        pl.semaphore_signal(barrier, inc=1, device_id=device, device_id_type=MESH)

    for d in range(1, NR):
        greet((f, ahead(d)))
    greet((mate, r))

    @pl.when(primary)
    def _():
        def greet_owner(t, carry):
            greet((2 * lax.rem(my_j + t, HALF) + par, r))
            return carry

        lax.fori_loop(1, HALF, greet_owner, 0, unroll=7)

    pl.semaphore_wait(barrier, jnp.where(primary, NR + HALF - 1, NR))

    load_g.wait()
    rs_copies = []
    for h in range(PARTS):
        row = []
        for d in range(1, NR):
            copy = remote(
                gv.at[pl.ds(ahead(d) * QB + h * PB, PB)],
                rs.at[d - 1, pl.ds(h * PB, PB)],
                rs_s.at[h, d - 1],
                rs_r.at[h, d - 1],
                (f, ahead(d)),
            )
            copy.start()
            row.append(copy)
        rs_copies.append(row)
    for i, row in enumerate(tables(owner_in[...], offset_in[...])):
        tabv[i : i + 1] = row
    for i in range(3, 8):
        tabv[i : i + 1] = jnp.zeros((1, 128), jnp.int32)
    table_copy = pltpu.make_async_copy(tabv, tab, tsem)
    table_copy.start()
    load_fac.wait()

    @pl.when(other)
    def _():
        fac_b[...] = fac[...].astype(BF16)

    def gather_copy(h, d, frm=None):
        base = (r if frm is None else frm) * QB + h * PB
        return remote(
            gq.at[pl.ds(h * PB, PB)],
            full.at[pl.ds(base, PB)],
            ag_s.at[h, d - 1],
            ag_r.at[h, d - 1],
            (f, ahead(d)),
        )

    table_copy.wait()
    for h in range(PARTS):
        here = pl.ds(h * PB, PB)
        for copy in rs_copies[h]:
            copy.wait_recv()
        total = gv[pl.ds(r * QB + h * PB, PB)].astype(F32)
        for d in range(1, NR):
            total = total + rs[d - 1, here].astype(F32)
        gq[here] = total.astype(BF16)
        for d in range(1, NR):
            gather_copy(h, d).start()
    full[pl.ds(r * QB, QB)] = gq[...]

    load_sec.wait()
    wide = gq[...].astype(F32)
    second = ADAM_DECAY * sec[...] + (1.0 - ADAM_DECAY) * wide * wide
    newsec[...] = second
    store_sec = pltpu.make_async_copy(newsec, newsec_out, osem.at[0])
    store_sec.start()
    direction = wide / (jnp.sqrt(second) + ADAM_EPS)
    lanes = jnp.sum(direction * direction, axis=1)
    sums = jnp.sum(lanes, axis=1, keepdims=True)
    diagonal = lax.broadcasted_iota(jnp.int32, (QB, 128), 0) == lax.broadcasted_iota(
        jnp.int32, (QB, 128), 1
    )
    row = jnp.sum(jnp.where(diagonal, sums, 0.0), axis=0, keepdims=True)
    prow[...] = jnp.broadcast_to(row, (8, 128))
    core_copy = remote(prow, cbuf, c_s, c_r, (mate, r))
    core_copy.start()

    for h in range(PARTS):
        for d in range(1, NR):
            gather_copy(h, d, behind(d)).wait_recv()

    @pl.when(other)
    def _():
        remote(fac_b, fac_x, fx_s, fx_r, (f, partner)).start()

    def chunk_for(j):
        owner = 2 * j + par
        column = tab[lax.div(owner, HALF), lax.rem(2 * owner + slot, NBLK)]
        return full[jnp.clip(column, 0, NBLK - 1)]

    far_first = (4, 5, 3, 6, 2, 7, 1, 0)

    def hand_over(d):
        rows = pl.ds(NZ * on_z(d), NZ)
        return remote(out.at[rows], comb.at[rows, f_par], l_s.at[d], l_r.at[d], (mate, r))

    def take_over(d):
        rows = pl.ds(NZ * on_z(d), NZ)
        part = comb.at[rows, 1 - f_par]
        return remote(out.at[rows], part, l_s.at[d], l_r.at[d], (mate, r))

    @pl.when(other)
    def _():
        for d in far_first:

            def build(y, carry, z=on_z(d)):
                out[NZ * z + y] = chunk_for(NZ * z + y)
                return carry

            lax.fori_loop(0, NZ, build, 0, unroll=True)
            hand_over(d).start()

    @pl.when(primary)
    def _():
        for d in far_first:

            def build(y, carry, z=on_z(d)):
                comb[NZ * z + y, f_par] = chunk_for(NZ * z + y)
                return carry

            lax.fori_loop(0, NZ, build, 0, unroll=True)
        for d in far_first:
            take_over(d).wait_recv()

            def send(e, carry, d=d):
                j = NZ * on_z(d) + on_y(e)
                remote(comb.at[j], arrived.at[my_j], a_s, a_r, (2 * j + par, r)).start()
                return carry

            lax.fori_loop(0 if d else 1, NZ, send, 0, unroll=True)
        arrived[my_j] = comb[my_j]

    def z_copy(d):
        return remote(zrow, zbuf.at[d - 1], z_s.at[d - 1], z_r.at[d - 1], along_z(d))

    def y_copy(d):
        return remote(yrow, ybuf.at[d - 1], y_s.at[d - 1], y_r.at[d - 1], along_y(d))

    def total_copy():
        return remote(trow, trow, t_s, t_r, (mate, r))

    core_copy.wait()
    weight = jnp.where(
        tab[lax.div(f, HALF), lax.rem(2 * f + slot, NBLK)] >= 0, 1.0 - FACTOR_DECAY, 0.0
    )
    all_but_one = pl.ds(0, HALF - 1)

    @pl.when(primary)
    def _():
        zrow[...] = prow[...] + cbuf[...]
        for d in range(1, NZ):
            z_copy(d).start()
        part = arrived.at[all_but_one]
        remote(part, part, a_s, a_r, (f, partner)).wait_recv()

    row_id = lax.broadcasted_iota(jnp.int32, (256, 256), 0)
    col_id = lax.broadcasted_iota(jnp.int32, (256, 256), 1)

    @pl.when(primary)
    def _():
        gather_id = ((row_id >> 2) & 15) * 16 + (row_id >> 6) * 4 + (row_id & 3)
        perm = jnp.where(col_id == gather_id, 1.0, 0.0).astype(BF16)
        for g in range(8):
            moved = dot32(perm, arrived[pl.ds(8 * g, 8)].reshape(256, 128)).astype(BF16)
            for q in range(4):
                block[pl.ds(64 * g, 64), pl.ds(128 * q, 128)] = moved[64 * q : 64 * q + 64]
        remote(block, block_x, gx_s, gx_r, (f, partner)).start()
        for d in range(1, NZ):
            z_copy(d).wait()
        acc = zrow[...]
        for d in range(1, NZ):
            acc = acc + zbuf[d - 1]
        yrow[...] = acc
        for d in range(1, NZ):
            y_copy(d).start()
        remote(fac_b, fac_x, fx_s, fx_r, (f, partner)).wait_recv()
    @pl.when(primary)
    def _():
        grad = block[...]
        own = fac[...]
        theirs = fac_x[...].astype(F32)
        is_left = par == 0
        left = FACTOR_DECAY * jnp.where(is_left, own, theirs) + weight * outer_left(grad)
        right = FACTOR_DECAY * jnp.where(is_left, theirs, own) + weight * outer_right(grad)
        newfac[...] = jnp.where(is_left, left, right)
        pltpu.make_async_copy(newfac, newfac_out, osem.at[1]).start()
        left_root, right_root = roots_of(
            [plus_diag(left, MATRIX_EPS), plus_diag(right, MATRIX_EPS)]
        )
        halfway = dot32(left_root, grad).astype(BF16)
        precond = dot32(halfway, right_root)
        prec_sq = jnp.sum(
            jnp.sum(precond * precond, axis=0, keepdims=True), axis=1, keepdims=True
        )
        unit = (precond * (1.0 / jnp.sqrt(prec_sq + NORM_EPS))).astype(BF16)
        unit_s[...] = unit

    def share():
        return remote(
            retpair.at[:, 1 - f_par], retpair.at[:, 1 - f_par], m_s, m_r, (mate, r)
        )

    @pl.when(primary)
    def _():
        scatter_id = ((row_id >> 2) & 3) * 64 + (row_id >> 4) * 4 + (row_id & 3)
        perm_back = jnp.where(col_id == scatter_id, 1.0, 0.0).astype(BF16)
        for d in far_first:
            rows = unit_s[pl.ds(64 * on_z(d), 64), :]
            piece = jnp.concatenate([rows[:, 128 * q : 128 * q + 128] for q in range(4)], axis=0)
            moved = dot32(perm_back, piece).astype(BF16).reshape(NZ, 2, 16, 128)
            ret[pl.ds(NZ * on_z(d), NZ)] = moved

            def send_back(e, carry, d=d):
                j = NZ * on_z(d) + on_y(e)
                remote(ret.at[j], retpair.at[my_j], b_s, b_r, (2 * j + par, r)).start()
                return carry

            lax.fori_loop(0 if d else 1, NZ, send_back, 0, unroll=True)
        retpair[my_j] = ret[my_j]
        for d in range(1, NZ):
            y_copy(d).wait()
        acc = yrow[...]
        for d in range(1, NZ):
            acc = acc + ybuf[d - 1]
        trow[...] = acc
        total_copy().start()
        part = retpair.at[all_but_one]
        remote(part, part, b_s, b_r, (f, partner)).wait_recv()
        share().start()

    @pl.when(other)
    def _():
        remote(block, block_x, gx_s, gx_r, (f, partner)).wait_recv()
        grad = block_x[...]

        @pl.when(par == 0)
        def _():
            newfac[...] = FACTOR_DECAY * fac[...] + weight * outer_left(grad)

        @pl.when(par == 1)
        def _():
            newfac[...] = FACTOR_DECAY * fac[...] + weight * outer_right(grad)

        pltpu.make_async_copy(newfac, newfac_out, osem.at[1]).start()
        total_copy().wait_recv()
        remote(retpair.at[:, f_par], retpair.at[:, f_par], m_s, m_r, (mate, r)).wait_recv()

    def back_for(column):
        s = tab[2, column]
        return retpair[s >> 2, f_par]

    for d in range(1, NR):
        base = ahead(d) * QB

        def pack(p, carry, d=d, base=base):
            xs[d - 1, p] = back_for(base + p)
            return carry

        lax.fori_loop(0, QB, pack, 0, unroll=8)
        remote(xs.at[d - 1], xr.at[r], x_s.at[d - 1], x_r.at[d - 1], (f, ahead(d))).start()

    def pack_own(p, carry):
        xr[r, p] = back_for(r * QB + p)
        return carry

    lax.fori_loop(0, QB, pack_own, 0, unroll=8)

    total_row = trow[0:1]
    scale = jnp.sqrt(
        jnp.sum(jnp.where(diagonal, total_row, 0.0), axis=1, keepdims=True)
    )
    load_mom.wait()
    decayed = MOMENTUM_DECAY * mom[...]
    newmom[...] = decayed
    for d in range(1, NR):
        part = xr.at[behind(d)]
        remote(xs.at[d - 1], part, x_s.at[d - 1], x_r.at[d - 1], (f, ahead(d))).wait_recv()
    for p in range(QB):
        s = tab[2, r * QB + p]
        holder = 2 * (s & 1) + ((s >> 1) & 1)
        newmom[p] = newmom[p] + xr[holder, p].astype(F32) * scale[p : p + 1]
    store_mom = pltpu.make_async_copy(newmom, newmom_out, osem.at[2])
    store_mom.start()

    for h in range(PARTS):
        for d in range(1, NR):
            rs_copies[h][d - 1].wait_send()
            gather_copy(h, d).wait_send()
    for d in range(1, NR):
        remote(xs.at[d - 1], xr.at[r], x_s.at[d - 1], x_r.at[d - 1], (f, ahead(d))).wait_send()

    @pl.when(primary)
    def _():
        part = comb.at[all_but_one]
        remote(part, part, a_s, a_r, (f, partner)).wait_send()
        part_b = ret.at[all_but_one]
        remote(part_b, part_b, b_s, b_r, (f, partner)).wait_send()
        remote(block, block_x, gx_s, gx_r, (f, partner)).wait_send()
        total_copy().wait_send()
        share().wait_send()

    @pl.when(other)
    def _():
        for d in far_first:
            hand_over(d).wait_send()
        remote(fac_b, fac_x, fx_s, fx_r, (f, partner)).wait_send()

    store_sec.wait()
    pltpu.make_async_copy(newfac, newfac_out, osem.at[1]).wait()
    store_mom.wait()


def place(*refs):
    *arrays, sems = refs
    count = len(arrays) // 3
    ins, outs, held = arrays[:count], arrays[count : 2 * count], arrays[2 * count :]
    loads = [pltpu.make_async_copy(ins[i], held[i], sems.at[0, i]) for i in range(count)]
    stores = [pltpu.make_async_copy(held[i], outs[i], sems.at[1, i]) for i in range(count)]
    for load in loads:
        load.start()
    for load, store in zip(loads, stores):
        load.wait()
        store.start()
    for store in stores:
        store.wait()


def chunked(array):
    columns = array.shape[1]
    tiles = array.reshape(4, columns // 128, 128).transpose(1, 0, 2)
    return tiles.reshape(columns // 512, 16, 128)


def unchunked(array):
    count = array.shape[0]
    return array.reshape(count * 4, 4, 128).transpose(1, 0, 2).reshape(4, count * 512)


def shards(replica_grads, momentum, second_moment, factor_stats, block_owner, block_offset):
    hbm = pl.BlockSpec(memory_space=pltpu.HBM)
    any_space = pl.BlockSpec(memory_space=pl.ANY)
    dma = pltpu.SemaphoreType.DMA
    outs = pl.pallas_call(
        kernel,
        out_shape=(
            jax.ShapeDtypeStruct((QB, 16, 128), F32),
            jax.ShapeDtypeStruct((QB, 16, 128), F32),
            jax.ShapeDtypeStruct((BS, BS), F32),
        ),
        in_specs=[pl.BlockSpec(memory_space=pltpu.VMEM)] * 2 + [hbm] * 4,
        out_specs=(any_space,) * 3,
        scratch_shapes=[
            pltpu.VMEM((QB, 16, 128), F32),
            pltpu.VMEM((QB, 16, 128), F32),
            pltpu.VMEM((BS, BS), F32),
            pltpu.VMEM((QB, 16, 128), F32),
            pltpu.VMEM((QB, 16, 128), F32),
            pltpu.VMEM((BS, BS), F32),
            pltpu.VMEM((NBLK, 16, 128), BF16),
            pltpu.VMEM((QB, 16, 128), BF16),
            pltpu.VMEM((NR - 1, QB, 16, 128), BF16),
            pltpu.VMEM((NBLK, 16, 128), BF16),
            pltpu.VMEM((HALF, 16, 128), BF16),
            pltpu.VMEM((HALF, 2, 16, 128), BF16),
            pltpu.VMEM((HALF, 2, 16, 128), BF16),
            pltpu.VMEM((BS, BS), BF16),
            pltpu.VMEM((BS, BS), BF16),
            pltpu.VMEM((BS, BS), BF16),
            pltpu.VMEM((BS, BS), BF16),
            pltpu.VMEM((BS, BS), BF16),
            pltpu.VMEM((HALF, 2, 16, 128), BF16),
            pltpu.VMEM((HALF, 2, 16, 128), BF16),
            pltpu.VMEM((NR - 1, QB, 16, 128), BF16),
            pltpu.VMEM((NR, QB, 16, 128), BF16),
            pltpu.VMEM((8, 128), F32),
            pltpu.VMEM((8, 128), F32),
            pltpu.VMEM((7, 8, 128), F32),
            pltpu.VMEM((8, 128), F32),
            pltpu.VMEM((7, 8, 128), F32),
            pltpu.VMEM((8, 128), F32),
            pltpu.VMEM((8, 128), F32),
            pltpu.VMEM((8, 128), jnp.int32),
            pltpu.SMEM((8, 128), jnp.int32),
            dma,
            dma((4,)),
            dma((3,)),
            dma((PARTS, 3)),
            dma((PARTS, 3)),
            dma((PARTS, 3)),
            dma((PARTS, 3)),
            dma,
            dma,
            dma,
            dma,
            dma,
            dma,
            dma,
            dma,
            dma((NZ,)),
            dma((NZ,)),
            dma,
            dma,
            dma,
            dma,
            dma((3,)),
            dma((3,)),
            dma((7,)),
            dma((7,)),
            dma((7,)),
            dma((7,)),
            dma,
            dma,
        ],
        compiler_params=pltpu.CompilerParams(
            collective_id=0, has_side_effects=True, vmem_limit_bytes=60 * 1024 * 1024
        ),
    )(
        block_owner.reshape(1, NBLK),
        block_offset.reshape(1, NBLK),
        chunked(replica_grads[0]),
        chunked(momentum),
        chunked(second_moment),
        factor_stats[0, 0],
    )
    count = len(outs)
    new_momentum, new_second, new_factors = pl.pallas_call(
        place,
        out_shape=[jax.ShapeDtypeStruct(o.shape, o.dtype) for o in outs],
        in_specs=[any_space] * count,
        out_specs=[any_space] * count,
        scratch_shapes=[pltpu.VMEM(o.shape, o.dtype) for o in outs] + [dma((2, count))],
        compiler_params=pltpu.CompilerParams(vmem_limit_bytes=60 * 1024 * 1024),
    )(*outs)
    return (unchunked(new_momentum), unchunked(new_second), new_factors[None, None])


def solution(mesh):
    placed = (
        P("rep", "fsdp", None),
        P("fsdp", "rep"),
        P("fsdp", "rep"),
        P("fsdp", "rep", None, None),
        P(),
        P(),
    )
    return jax.shard_map(
        shards,
        mesh=mesh,
        in_specs=placed,
        out_specs=(P("fsdp", "rep"), P("fsdp", "rep"), P("fsdp", "rep", None, None)),
        check_vma=False,
    )
```

time: 81.5 us -> 71.3 us (0.87)
  local copies, waits for them, and re-layouts: 7.67 us -> 0 us
  Pallas kernels: 72.5 us -> 70.5 us
    unnamed x15 -> x0, local copies, waits for them, and re-layouts: 7.67 us -> none
    pallas_call x1, Pallas kernels: 72.5 us -> 68.1 us  [shards(): pl.pallas_call(kernel, out_shape=(jax.ShapeDtypeStruct((QB, 16, 128), F32...]
    pallas_call x0 -> x1, Pallas kernels: none -> 2.41 us  [shards(): pl.pallas_call(place, out_shape=[jax.ShapeDtypeStruct(o.shape, o.dtype) f...]
where the time goes in v2:
time: 71.3 us; the launch traced here: 71.1 us
  Pallas kernels  70.5 us (99%)
    pallas_call x1, Pallas kernels, shards(): pl.pallas_call(kernel, out_shape=(jax.ShapeDtypeStruct((QB, 16, 128), F32...  68.1 us
    pallas_call x1, Pallas kernels, shards(): pl.pallas_call(place, out_shape=[jax.ShapeDtypeStruct(o.shape, o.dtype) f...  2.41 us

profile of v2, /device:TPU:1, one launch (start us, length us, event | category | flops | bytes accessed | tf_op | source)
XLA Modules:
  0.0 71.1 jit_solution(1844759428678139511)
XLA Ops:
  0.6 68.1 %shard_map.85 = (f32[32,16,128]{2,1,0:T(8,128)}, f32[32,16,128]{2,1,0:T(8,128)}, f32[512,512]{1,0:T(8,128)}) custom-call(s32[1,128]{1,0:T(1,128)} %bitcast.33, s32[1,128]{1,0:T(1,128)} %bitcast.34, bf16[128,16,128]{2,1,0:T(8,128)(2,1)} %bitcast.30, f32[32,16,128]{2,1,0:T(8,128)} %bitcast.31, f32[32,16,128]{2,1,0:T(8,128)} %bitcast.32, f32[512,512]{1,0:T(8,128)} %bitcast.29), custom_call_target="tpu_custom_call" | custom-call | tf_op jit(solution)/shard_map/pallas_call | solution.py:574
  68.7 2.4 %shard_map.86 = (f32[32,16,128]{2,1,0:T(8,128)}, f32[32,16,128]{2,1,0:T(8,128)}, f32[512,512]{1,0:T(8,128)}) custom-call(f32[32,16,128]{2,1,0:T(8,128)} %get-tuple-element.9.refs_0_, f32[32,16,128]{2,1,0:T(8,128)} %get-tuple-element.10.refs_1_, f32[512,512]{1,0:T(8,128)} %get-tuple-element.11.refs_2_), custom_call_target="tpu_custom_call" | custom-call | tf_op jit(solution)/shard_map/pallas_call | solution.py:657

commit v3 on v2

--- a/solution.py
+++ b/solution.py
@@ -51,14 +51,12 @@
 def roots_of(mats):
     norms = [jnp.sum(jnp.sum(m * m, axis=0, keepdims=True), axis=1, keepdims=True) for m in mats]
     scales = [2.5 / jnp.sqrt(n) for n in norms]
-    coupled0 = [z * m for z, m in zip(scales, mats)]
+    coupled0 = [(0.25 * z) * m for z, m in zip(scales, mats)]
 
     def next_coupled(coupled, rounded):
-        square = [dot32(m, m) for m in rounded]
-        inner = [s * 0.0625 - 0.625 * m for s, m in zip(square, coupled)]
+        inner = [dot32(m, m) - 2.5 * c for m, c in zip(rounded, coupled)]
         inner_b = [e.astype(BF16) for e in inner]
-        fourth = [dot32(e, e) for e in inner_b]
-        rest = [(q + 3.125 * e).astype(BF16) for q, e in zip(fourth, inner)]
+        rest = [(dot32(b, b) + 3.125 * e).astype(BF16) for b, e in zip(inner_b, inner)]
         return [
             dot32(w, m) + (625.0 / 256.0) * c for w, m, c in zip(rest, rounded, coupled)
         ]
@@ -67,14 +65,14 @@
     coupled1 = next_coupled(coupled0, rounded0)
     rounded1 = [m.astype(BF16) for m in coupled1]
     pair = [
-        (dot32(a, b) - 5.0 * (c + d)) * 0.0625
+        dot32(a, b) - 1.25 * (c + d)
         for a, b, c, d in zip(rounded0, rounded1, coupled0, coupled1)
     ]
     coupled2 = next_coupled(coupled1, rounded1)
     out = []
     for u, m, z in zip(pair, coupled2, scales):
-        last = 5.0 * u - (25.0 / 16.0) * m - dot32(u.astype(BF16), m.astype(BF16))
-        root = plus_diag(last * 0.25, 125.0 / 64.0) * jnp.sqrt(jnp.sqrt(z))
+        last = 1.25 * u - 1.5625 * m - dot32(u.astype(BF16), m.astype(BF16))
+        root = plus_diag(last, 125.0 / 64.0) * jnp.sqrt(jnp.sqrt(z))
         out.append(root.astype(BF16))
     return out
 
@@ -243,7 +241,7 @@
     rs_copies = []
     for h in range(PARTS):
         row = []
-        for d in range(1, NR):
+        for d in (2, 1, 3):
             copy = remote(
                 gv.at[pl.ds(ahead(d) * QB + h * PB, PB)],
                 rs.at[d - 1, pl.ds(h * PB, PB)],
@@ -285,7 +283,7 @@
         for d in range(1, NR):
             total = total + rs[d - 1, here].astype(F32)
         gq[here] = total.astype(BF16)
-        for d in range(1, NR):
+        for d in (2, 1, 3):
             gather_copy(h, d).start()
     full[pl.ds(r * QB, QB)] = gq[...]
 
@@ -323,11 +321,11 @@
 
     def hand_over(d):
         rows = pl.ds(NZ * on_z(d), NZ)
-        return remote(out.at[rows], comb.at[rows, f_par], l_s.at[d], l_r.at[d], (mate, r))
+        return remote(out.at[rows], comb.at[f_par, rows], l_s.at[d], l_r.at[d], (mate, r))
 
     def take_over(d):
         rows = pl.ds(NZ * on_z(d), NZ)
-        part = comb.at[rows, 1 - f_par]
+        part = comb.at[1 - f_par, rows]
         return remote(out.at[rows], part, l_s.at[d], l_r.at[d], (mate, r))
 
     @pl.when(other)
@@ -346,7 +344,7 @@
         for d in far_first:
 
             def build(y, carry, z=on_z(d)):
-                comb[NZ * z + y, f_par] = chunk_for(NZ * z + y)
+                comb[f_par, NZ * z + y] = chunk_for(NZ * z + y)
                 return carry
 
             lax.fori_loop(0, NZ, build, 0, unroll=True)
@@ -355,11 +353,11 @@
 
             def send(e, carry, d=d):
                 j = NZ * on_z(d) + on_y(e)
-                remote(comb.at[j], arrived.at[my_j], a_s, a_r, (2 * j + par, r)).start()
+                remote(comb.at[:, j], arrived.at[my_j], a_s, a_r, (2 * j + par, r)).start()
                 return carry
 
             lax.fori_loop(0 if d else 1, NZ, send, 0, unroll=True)
-        arrived[my_j] = comb[my_j]
+        arrived[my_j] = comb[:, my_j]
 
     def z_copy(d):
         return remote(zrow, zbuf.at[d - 1], z_s.at[d - 1], z_r.at[d - 1], along_z(d))
@@ -428,7 +426,7 @@
 
     def share():
         return remote(
-            retpair.at[:, 1 - f_par], retpair.at[:, 1 - f_par], m_s, m_r, (mate, r)
+            retpair.at[1 - f_par], retpair.at[1 - f_par], m_s, m_r, (mate, r)
         )
 
     @pl.when(primary)
@@ -443,11 +441,11 @@
 
             def send_back(e, carry, d=d):
                 j = NZ * on_z(d) + on_y(e)
-                remote(ret.at[j], retpair.at[my_j], b_s, b_r, (2 * j + par, r)).start()
+                remote(ret.at[j], retpair.at[:, my_j], b_s, b_r, (2 * j + par, r)).start()
                 return carry
 
             lax.fori_loop(0 if d else 1, NZ, send_back, 0, unroll=True)
-        retpair[my_j] = ret[my_j]
+        retpair[:, my_j] = ret[my_j]
         for d in range(1, NZ):
             y_copy(d).wait()
         acc = yrow[...]
@@ -455,7 +453,7 @@
             acc = acc + ybuf[d - 1]
         trow[...] = acc
         total_copy().start()
-        part = retpair.at[all_but_one]
+        part = ret.at[all_but_one]
         remote(part, part, b_s, b_r, (f, partner)).wait_recv()
         share().start()
 
@@ -474,13 +472,13 @@
 
         pltpu.make_async_copy(newfac, newfac_out, osem.at[1]).start()
         total_copy().wait_recv()
-        remote(retpair.at[:, f_par], retpair.at[:, f_par], m_s, m_r, (mate, r)).wait_recv()
+        remote(retpair.at[f_par], retpair.at[f_par], m_s, m_r, (mate, r)).wait_recv()
 
     def back_for(column):
         s = tab[2, column]
-        return retpair[s >> 2, f_par]
-
-    for d in range(1, NR):
+        return retpair[f_par, s >> 2]
+
+    for d in (2, 1, 3):
         base = ahead(d) * QB
 
         def pack(p, carry, d=d, base=base):
@@ -515,14 +513,14 @@
 
     for h in range(PARTS):
         for d in range(1, NR):
-            rs_copies[h][d - 1].wait_send()
+            rs_copies[h][(1, 0, 2)[d - 1]].wait_send()
             gather_copy(h, d).wait_send()
     for d in range(1, NR):
         remote(xs.at[d - 1], xr.at[r], x_s.at[d - 1], x_r.at[d - 1], (f, ahead(d))).wait_send()
 
     @pl.when(primary)
     def _():
-        part = comb.at[all_but_one]
+        part = arrived.at[all_but_one]
         remote(part, part, a_s, a_r, (f, partner)).wait_send()
         part_b = ret.at[all_but_one]
         remote(part_b, part_b, b_s, b_r, (f, partner)).wait_send()
@@ -592,7 +590,7 @@
             pltpu.VMEM((NR - 1, QB, 16, 128), BF16),
             pltpu.VMEM((NBLK, 16, 128), BF16),
             pltpu.VMEM((HALF, 16, 128), BF16),
-            pltpu.VMEM((HALF, 2, 16, 128), BF16),
+            pltpu.VMEM((2, HALF, 16, 128), BF16),
             pltpu.VMEM((HALF, 2, 16, 128), BF16),
             pltpu.VMEM((BS, BS), BF16),
             pltpu.VMEM((BS, BS), BF16),
@@ -600,7 +598,7 @@
             pltpu.VMEM((BS, BS), BF16),
             pltpu.VMEM((BS, BS), BF16),
             pltpu.VMEM((HALF, 2, 16, 128), BF16),
-            pltpu.VMEM((HALF, 2, 16, 128), BF16),
+            pltpu.VMEM((2, HALF, 16, 128), BF16),
             pltpu.VMEM((NR - 1, QB, 16, 128), BF16),
             pltpu.VMEM((NR, QB, 16, 128), BF16),
             pltpu.VMEM((8, 128), F32),

time: 71.3 us -> 68.7 us (0.964)
  Pallas kernels: 70.5 us -> 67.8 us
    pallas_call x1, Pallas kernels: 68.1 us -> 65.4 us  [shards(): pl.pallas_call(kernel, out_shape=(jax.ShapeDtypeStruct((QB, 16, 128), F32...]
where the time goes in v3:
time: 68.7 us; the launch traced here: 68.5 us
  Pallas kernels  67.8 us (99%)
    pallas_call x1, Pallas kernels, shards(): pl.pallas_call(kernel, out_shape=(jax.ShapeDtypeStruct((QB, 16, 128), F32...  65.4 us
    pallas_call x1, Pallas kernels, shards(): pl.pallas_call(place, out_shape=[jax.ShapeDtypeStruct(o.shape, o.dtype) f...  2.41 us

profile of v3, /device:TPU:1, one launch (start us, length us, event | category | flops | bytes accessed | tf_op | source)
XLA Modules:
  0.0 68.5 jit_solution(9463871730456467504)
XLA Ops:
  0.6 65.4 %shard_map.85 = (f32[32,16,128]{2,1,0:T(8,128)}, f32[32,16,128]{2,1,0:T(8,128)}, f32[512,512]{1,0:T(8,128)}) custom-call(s32[1,128]{1,0:T(1,128)} %bitcast.33, s32[1,128]{1,0:T(1,128)} %bitcast.34, bf16[128,16,128]{2,1,0:T(8,128)(2,1)} %bitcast.30, f32[32,16,128]{2,1,0:T(8,128)} %bitcast.31, f32[32,16,128]{2,1,0:T(8,128)} %bitcast.32, f32[512,512]{1,0:T(8,128)} %bitcast.29), custom_call_target="tpu_custom_call" | custom-call | tf_op jit(solution)/shard_map/pallas_call | solution.py:572
  66.1 2.4 %shard_map.86 = (f32[32,16,128]{2,1,0:T(8,128)}, f32[32,16,128]{2,1,0:T(8,128)}, f32[512,512]{1,0:T(8,128)}) custom-call(f32[32,16,128]{2,1,0:T(8,128)} %get-tuple-element.9.refs_0_, f32[32,16,128]{2,1,0:T(8,128)} %get-tuple-element.10.refs_1_, f32[512,512]{1,0:T(8,128)} %get-tuple-element.11.refs_2_), custom_call_target="tpu_custom_call" | custom-call | tf_op jit(solution)/shard_map/pallas_call | solution.py:655

commit v4 on v3

--- a/solution.py
+++ b/solution.py
@@ -308,10 +308,6 @@
         for d in range(1, NR):
             gather_copy(h, d, behind(d)).wait_recv()
 
-    @pl.when(other)
-    def _():
-        remote(fac_b, fac_x, fx_s, fx_r, (f, partner)).start()
-
     def chunk_for(j):
         owner = 2 * j + par
         column = tab[lax.div(owner, HALF), lax.rem(2 * owner + slot, NBLK)]
@@ -338,6 +334,7 @@
 
             lax.fori_loop(0, NZ, build, 0, unroll=True)
             hand_over(d).start()
+        remote(fac_b, fac_x, fx_s, fx_r, (f, partner)).start()
 
     @pl.when(primary)
     def _():

time: 68.7 us -> 68.7 us (level)
  no operation moved by 1% of the time
where the time goes in v4:
time: 68.7 us; the launch traced here: 68.1 us
  Pallas kernels  67.5 us (98%)
    pallas_call x1, Pallas kernels, shards(): pl.pallas_call(kernel, out_shape=(jax.ShapeDtypeStruct((QB, 16, 128), F32...  65 us
    pallas_call x1, Pallas kernels, shards(): pl.pallas_call(place, out_shape=[jax.ShapeDtypeStruct(o.shape, o.dtype) f...  2.41 us

profile of v4, /device:TPU:1, one launch (start us, length us, event | category | flops | bytes accessed | tf_op | source)
XLA Modules:
  0.0 68.1 jit_solution(11257880911786703283)
XLA Ops:
  0.6 65.0 %shard_map.85 = (f32[32,16,128]{2,1,0:T(8,128)}, f32[32,16,128]{2,1,0:T(8,128)}, f32[512,512]{1,0:T(8,128)}) custom-call(s32[1,128]{1,0:T(1,128)} %bitcast.33, s32[1,128]{1,0:T(1,128)} %bitcast.34, bf16[128,16,128]{2,1,0:T(8,128)(2,1)} %bitcast.30, f32[32,16,128]{2,1,0:T(8,128)} %bitcast.31, f32[32,16,128]{2,1,0:T(8,128)} %bitcast.32, f32[512,512]{1,0:T(8,128)} %bitcast.29), custom_call_target="tpu_custom_call" | custom-call | tf_op jit(solution)/shard_map/pallas_call | solution.py:569
  65.7 2.4 %shard_map.86 = (f32[32,16,128]{2,1,0:T(8,128)}, f32[32,16,128]{2,1,0:T(8,128)}, f32[512,512]{1,0:T(8,128)}) custom-call(f32[32,16,128]{2,1,0:T(8,128)} %get-tuple-element.9.refs_0_, f32[32,16,128]{2,1,0:T(8,128)} %get-tuple-element.10.refs_1_, f32[512,512]{1,0:T(8,128)} %get-tuple-element.11.refs_2_), custom_call_target="tpu_custom_call" | custom-call | tf_op jit(solution)/shard_map/pallas_call | solution.py:652
